TPU v7x, 32 devices: a whole 2x2x4 slice. The times are simulated.
32 devices in a mesh: rep: 2 (over x), node: 2 (over core), local: 8 (over z, y).
Axes of the slice: x: 2, y: 2, z: 4, core: 2. Of those that a mesh axis runs over, the one named last changes fastest.
Arguments:
- hidden_rows: bfloat16 [256, 7168], P(('rep', 'node', 'local')), parts along dimension 0, may hold values from -6 to 6
- w_router: bfloat16 [7168, 8], replicated, may hold values from -0.0625 to 0.0625
- chosen: int32 [256, 4], P(('rep', 'node', 'local')), parts along dimension 0, may hold values from 0 to 7, all different within a row; in each aligned block of 8 rows (0 to 7, 8 to 15, ...) at most 6 rows name the same one
- w_gate: bfloat16 [7168, 16384], P(None, ('node', 'local')), may hold values from -0.0625 to 0.0625
- w_up: bfloat16 [7168, 16384], P(None, ('node', 'local')), may hold values from -0.0625 to 0.0625
- w_down: bfloat16 [16384, 7168], P(('node', 'local')), may hold values from -0.125 to 0.125
- q_latent: bfloat16 [64, 65536], P(('rep', 'node', 'local')), parts along dimension 0, may hold values from -73 to 73
- q_rope: bfloat16 [64, 8192], P(('rep', 'node', 'local')), parts along dimension 0, may hold values from -4 to 4
- cache_latent: bfloat16 [64, 512, 512], P(('rep', 'node', 'local')), parts along dimension 0, may hold values from -4 to 4
- cache_rope: bfloat16 [64, 64, 512], P(('rep', 'node', 'local')), parts along dimension 0, may hold values from -4 to 4
- lengths: int32 [64], P(('rep', 'node', 'local')), parts along dimension 0, may hold values from 64 to 512, as said below
Outputs:
- moe_out: bfloat16 [256, 7168], P(('rep', 'node', 'local')), parts along dimension 0
- context: bfloat16 [64, 65536], P(('rep', 'node', 'local')), parts along dimension 0
There are 2 independent parts, one for each index of `rep`. A program takes and returns all parts, laid end to end along the dimension named above; an argument that names none is the same for every part. Nothing has to cross between parts.
Inputs may be any that keep to these rules, and one draw needn't show every extreme that they name: `chosen`: each row names 4 different experts; among the rows of one device no expert is named by more than 6 rows, a bound that some block reaches. `lengths`: some row has all 512 positions filled.
All inputs are finite; a program needn't handle non-finite values.
Results may differ from a plain program's by a relative error of at most 0.005.
Values may be sent and summed in bfloat16 or wider, within the bound.
A program may use at most 128 MiB of HBM per device.

v0:
```python
import jax
import jax.numpy as jnp
from jax import lax
from jax.sharding import PartitionSpec as P

NG = 8
CAP = 6


route_scale = 2.5
score_scale = 192.0 ** (-0.5)


def expert_part(received, w_gate, w_up, w_down):
    model_width = received.shape[-1]
    flat_rows = received.reshape(-1, model_width)
    gate_act = jnp.dot(flat_rows, w_gate, preferred_element_type=jnp.float32)
    up_act = jnp.dot(flat_rows, w_up, preferred_element_type=jnp.float32)
    inner_act = (jax.nn.silu(gate_act) * up_act).astype(jnp.bfloat16)
    partial_out = jnp.dot(inner_act, w_down, preferred_element_type=jnp.float32)
    return partial_out.reshape(received.shape)


def attend(q_latent, q_rope, cache_latent, cache_rope, lengths):
    batch_rows, positions, latent = cache_latent.shape
    rope_width = cache_rope.shape[1]
    head_count = q_latent.shape[1] // latent
    queries = q_latent.reshape(batch_rows, head_count, latent)
    rope_queries = q_rope.reshape(batch_rows, head_count, rope_width)
    logits = jnp.einsum("bhl,btl->bht", queries, cache_latent, preferred_element_type=jnp.float32)
    logits = logits + jnp.einsum(
        "bhr,brt->bht", rope_queries, cache_rope, preferred_element_type=jnp.float32
    )
    logits = logits * score_scale
    usable = lax.broadcasted_iota(jnp.int32, (batch_rows, 1, positions), 2) < lengths[:, None, None]
    logits = jnp.where(usable, logits, -1e30)
    row_peak = jnp.max(logits, axis=2, keepdims=True)
    raw_weights = jnp.exp(logits - row_peak)
    attn_probs = (raw_weights / jnp.sum(raw_weights, axis=2, keepdims=True)).astype(jnp.bfloat16)
    summed = jnp.einsum(
        "bht,btl->bhl", attn_probs, cache_latent, preferred_element_type=jnp.float32
    )
    return summed.reshape(batch_rows, head_count * latent).astype(jnp.bfloat16)


def local(
    hidden_rows,
    w_router,
    chosen,
    w_gate,
    w_up,
    w_down,
    q_latent,
    q_rope,
    cache_latent,
    cache_rope,
    lengths,
):
    context = attend(q_latent, q_rope, cache_latent, cache_rope, lengths)
    row_count, model_width = hidden_rows.shape
    node_count = lax.axis_size("node")
    local_count = lax.axis_size("local")
    per_node = NG // node_count
    expert_span = local_count // per_node
    scores = jax.nn.sigmoid(jnp.dot(hidden_rows, w_router, preferred_element_type=jnp.float32))
    member = chosen[:, :, None] == lax.broadcasted_iota(jnp.int32, (1, 1, NG), 2)
    picked = jnp.sum(jnp.where(member, scores[:, None, :], 0.0), axis=2)
    weights = route_scale * picked / jnp.sum(picked, axis=1, keepdims=True)
    counts = jnp.sum(member.astype(jnp.int32), axis=1)
    before = jnp.cumsum(counts, axis=0) - counts
    slot_index = jnp.sum(jnp.where(member, before[:, None, :], 0), axis=2)
    target = chosen * CAP + slot_index
    placing = lax.broadcasted_iota(jnp.int32, (NG * CAP, 1, 1), 0) == target[None, :, :]
    placing = jnp.any(placing, axis=2).astype(jnp.bfloat16)
    outgoing = jnp.dot(placing, hidden_rows, preferred_element_type=jnp.float32).astype(
        jnp.bfloat16
    )
    outgoing = outgoing.reshape(NG, CAP, model_width)
    paired = lax.all_to_all(
        outgoing.reshape(node_count, per_node * CAP, model_width),
        "node",
        split_axis=0,
        concat_axis=0,
        tiled=True,
    )
    paired = paired.reshape(node_count, per_node, CAP, model_width)
    fanned = jnp.repeat(paired, expert_span, axis=1)
    received = lax.all_to_all(fanned, "local", split_axis=1, concat_axis=1, tiled=True)
    partial_out = expert_part(received, w_gate, w_up, w_down)
    returned = lax.all_to_all(partial_out, "local", split_axis=1, concat_axis=1, tiled=True)
    slot_count = received.shape[2]
    reduced = jnp.sum(
        returned.reshape(node_count, per_node, expert_span, slot_count, model_width), axis=2
    )
    gathered = lax.all_to_all(reduced, "node", split_axis=0, concat_axis=0, tiled=True)
    gathered = gathered.reshape(NG * CAP, model_width)
    picks = jnp.take(gathered, target.reshape(-1), axis=0).reshape(
        row_count, target.shape[1], model_width
    )
    mixed_sum = jnp.sum(weights[:, :, None] * picks, axis=1)
    moe_out = mixed_sum.astype(jnp.bfloat16)
    return (moe_out, context)


def solution(mesh):
    return jax.shard_map(
        local,
        mesh=mesh,
        in_specs=(
            P(("rep", "node", "local"), None),
            P(),
            P(("rep", "node", "local"), None),
            P(None, ("node", "local")),
            P(None, ("node", "local")),
            P(("node", "local"), None),
            P(("rep", "node", "local"), None),
            P(("rep", "node", "local"), None),
            P(("rep", "node", "local"), None, None),
            P(("rep", "node", "local"), None, None),
            P(("rep", "node", "local")),
        ),
        out_specs=(P(("rep", "node", "local"), None), P(("rep", "node", "local"), None)),
        check_vma=False,
    )
```

profile of v0, /device:TPU:0, one launch (start us, length us, event | category | flops | bytes accessed | tf_op | source)
XLA Modules:
  0.0 168.1 jit_solution(4198627080855682875)
XLA Ops:
  0.6 0.8 convert_reduce_fusion
  1.5 0.9 select_reduce_fusion.2
  2.4 0.7 compare_and_fusion
  3.2 1.3 convolution_convert_fusion
  4.5 4.3 %all_to_all.20 = bf16[2,24,7168]{2,1,0:T(8,128)(2,1)S(1)} all-to-all(bf16[2,24,7168]{2,1,0:T(8,128)(2,1)S(1)} %bitcast.30), channel_id=1, replica_groups=mesh['rep'=2,'node'=2,'local'=8] {'node'}, dimensions={0} | all-to-all | bytes 1376256 | tf_op jit(solution)/shard_map/all_to_all | solution.py:79
  8.7 0.7 copy.46
  9.5 0.7 broadcast_in_dim.63
  10.2 40.8 %all_to_all.21 = bf16[2,8,6,7168]{3,0,2,1:T(2,128)(2,1)S(1)} all-to-all(bf16[2,8,6,7168]{3,0,2,1:T(2,128)(2,1)S(1)} %bitcast.29), channel_id=1, replica_groups=mesh['rep'=2,'node'=2,'local'=8] {'local'}, dimensions={1} | all-to-all | bytes 2752512 | tf_op jit(solution)/shard_map/all_to_all | solution.py:88
  50.9 1.6 copy.47
  52.5 1.7 %reshape.126 = bf16[96,7168]{1,0:T(8,128)(2,1)S(1)} reshape(bf16[2,8,6,7168]{3,2,1,0:T(8,128)(2,1)} %copy.47) | data formatting | bytes 2752512 | tf_op jit(solution)/shard_map/reshape | solution.py:16
  54.2 7.6 %fusion.25 = f32[96,1024]{1,0:T(8,128)S(1)} fusion(bf16[96,7168]{1,0:T(8,128)(2,1)S(1)} %reshape.126, bf16[7168,1024]{1,0:T(8,128)(2,1)} %param.14), kind=kOutput, calls=%fused_computation.47 | convolution fusion | flops 1409286144 | bytes 16449536 | tf_op jit(solution)/shard_map/dot_general | solution.py:17
  61.9 15.7 %fusion.10 = f32[96,7168]{1,0:T(8,128)} fusion(bf16[1024,7168]{1,0:T(8,128)(2,1)} %param.16, bf16[96,7168]{1,0:T(8,128)(2,1)S(1)} %reshape.126, bf16[7168,1024]{1,0:T(8,128)(2,1)} %param.15, f32[96,1024]{1,0:T(8,128)S(1)} %fusion.25), kind=kOutput, calls=%fused_computation.18 | convolution fusion | flops 2819162112 | bytes 33882112 | tf_op jit(solution)/shard_map/dot_general | solution.py:20
  77.6 3.3 %reshape.127 = f32[2,8,6,7168]{3,2,1,0:T(8,128)} reshape(f32[96,7168]{1,0:T(8,128)} %fusion.10) | data formatting | bytes 5505024 | tf_op jit(solution)/shard_map/reshape | solution.py:21
  80.9 5.7 %copy.48 = f32[2,8,6,7168]{3,0,2,1:T(2,128)} copy(f32[2,8,6,7168]{3,2,1,0:T(8,128)} %reshape.127) | data formatting | bytes 5505024 | tf_op jit(solution)/shard_map/reshape | solution.py:21
  86.6 4.7 %all-to-all-start.2 = ((f32[2,8,6,7168]{3,0,2,1:T(2,128)}), f32[2,8,6,7168]{3,0,2,1:T(2,128)}, u32[]{:S(2)}, u32[]{:S(2)}) async-start(f32[2,8,6,7168]{3,0,2,1:T(2,128)} %copy.48), calls=%async_computation.2 | async-start | bytes 5505024 | tf_op jit(solution)/shard_map/all_to_all | solution.py:90
  93.9 1.0 copy.55
  94.8 57.6 %all-to-all-done.2 = f32[2,8,6,7168]{3,0,2,1:T(2,128)} async-done(((f32[2,8,6,7168]{3,0,2,1:T(2,128)}), f32[2,8,6,7168]{3,0,2,1:T(2,128)}, u32[]{:S(2)}, u32[]{:S(2)}) %all-to-all-start.2) | async-done | bytes 2752544 | tf_op jit(solution)/shard_map/all_to_all | solution.py:90
  152.5 3.6 %bitcast_reduce_fusion = f32[2,4,6,7168]{3,0,2,1:T(2,128)S(1)} fusion(f32[2,8,6,7168]{3,0,2,1:T(2,128)} %all-to-all-done.2), kind=kLoop, calls=%fused_computation.3 | loop fusion | flops 344064 | bytes 4128768 | tf_op jit(solution)/shard_map/reduce_sum | solution.py:92
  156.1 0.9 copy.49
  157.0 4.8 %all_to_all.22 = f32[2,4,6,7168]{3,1,2,0:T(4,128)S(1)} all-to-all(f32[2,4,6,7168]{3,1,2,0:T(4,128)S(1)} %copy.49), channel_id=1, replica_groups=mesh['rep'=2,'node'=2,'local'=8] {'node'}, dimensions={0} | all-to-all | bytes 2752512 | tf_op jit(solution)/shard_map/all_to_all | solution.py:95
  161.8 2.1 %copy.50 = f32[2,4,6,7168]{3,2,1,0:T(8,128)} copy(f32[2,4,6,7168]{3,1,2,0:T(4,128)S(1)} %all_to_all.22) | data formatting | bytes 2752512 | tf_op jit(solution)/shard_map/all_to_all | solution.py:95
  163.9 1.7 %reshape.129 = f32[48,7168]{1,0:T(8,128)S(1)} reshape(f32[2,4,6,7168]{3,2,1,0:T(8,128)} %copy.50) | data formatting | bytes 2752512 | tf_op jit(solution)/shard_map/reshape | solution.py:96
  165.6 0.9 gather_fusion
  166.7 1.3 multiply_reduce_fusion
  (35 shorter events, 2.8 us)
Async XLA Ops:
  0.6 91.9 %copy-start = (bf16[2,512,512]{2,1,0:T(8,128)(2,1)S(1)}, bf16[2,512,512]{2,1,0:T(8,128)(2,1)}, u32[]{:S(2)}) copy-start(bf16[2,512,512]{2,1,0:T(8,128)(2,1)} %param.19) | copy-start | bytes 3145732
  86.6 5.0 %copy-start.1 = (bf16[8,7168]{1,0:T(8,128)(2,1)S(1)}, bf16[8,7168]{1,0:T(8,128)(2,1)}, u32[]{:S(2)}) copy-start(bf16[8,7168]{1,0:T(8,128)(2,1)} %param.11) | copy-start | bytes 344068
  86.6 5.0 %copy-start.4 = (bf16[7168,8]{0,1:T(8,128)(2,1)S(1)}, bf16[7168,8]{0,1:T(8,128)(2,1)}, u32[]{:S(2)}) copy-start(bf16[7168,8]{0,1:T(8,128)(2,1)} %param.12) | copy-start | bytes 344068
  86.6 5.2 %copy-start.6 = (s32[8,4]{0,1:T(4,128)S(1)}, s32[8,4]{0,1:T(4,128)}, u32[]{:S(2)}) copy-start(s32[8,4]{0,1:T(4,128)} %param.13) | copy-start | bytes 388
  86.6 5.5 %copy-start.5 = (bf16[2,8192]{1,0:T(2,128)(2,1)S(1)}, bf16[2,8192]{1,0:T(2,128)(2,1)}, u32[]{:S(2)}) copy-start(bf16[2,8192]{1,0:T(2,128)(2,1)} %param.18) | copy-start | bytes 98308
  86.6 5.7 %copy-start.7 = (s32[2]{0:T(128)S(1)}, s32[2]{0:T(128)}, u32[]{:S(2)}) copy-start(s32[2]{0:T(128)} %param.21) | copy-start | bytes 28
  86.6 5.7 %copy-start.3 = (bf16[2,64,512]{2,1,0:T(8,128)(2,1)S(1)}, bf16[2,64,512]{2,1,0:T(8,128)(2,1)}, u32[]{:S(2)}) copy-start(bf16[2,64,512]{2,1,0:T(8,128)(2,1)} %param.20) | copy-start | bytes 393220
  86.6 5.9 %copy-start.2 = (bf16[2,65536]{1,0:T(2,128)(2,1)S(1)}, bf16[2,65536]{1,0:T(2,128)(2,1)}, u32[]{:S(2)}) copy-start(bf16[2,65536]{1,0:T(2,128)(2,1)} %param.17) | copy-start | bytes 786436
  86.6 65.8 %all-to-all-start.2 = ((f32[2,8,6,7168]{3,0,2,1:T(2,128)}), f32[2,8,6,7168]{3,0,2,1:T(2,128)}, u32[]{:S(2)}, u32[]{:S(2)}) async-start(f32[2,8,6,7168]{3,0,2,1:T(2,128)} %copy.48), calls=%async_computation.2 | async-start | bytes 5505024 | tf_op jit(solution)/shard_map/all_to_all | solution.py:90
where the time goes:
time: 169 us; the launch traced here: 168 us
  waiting for transfers between devices  57.6 us (34%)
  blocking collectives  49.9 us (30%)
  matrix products  26 us (15%)
  local copies, waits for them, and re-layouts  21 us (12%)
  other arithmetic  8.04 us (5%)
  starting transfers between devices  4.72 us (3%)
    all_to_all x1, waiting for transfers between devices, local(): lax.all_to_all(partial_out, 'local', split_axis=1, concat_axis=1, tiled=T...  57.6 us
    all_to_all x1, blocking collectives, local(): lax.all_to_all(fanned, 'local', split_axis=1, concat_axis=1, tiled=True)  40.8 us
    dot_general x1, matrix products, expert_part(): partial_out = jnp.dot(inner_act, w_down, preferred_element_type=jnp.float32)  15.7 us
    reshape x2, local copies, waits for them, and re-layouts, expert_part(): return partial_out.reshape(received.shape)  9.01 us
    dot_general x1, matrix products, expert_part(): gate_act = jnp.dot(flat_rows, w_gate, preferred_element_type=jnp.float32)  7.61 us
    all_to_all x1, blocking collectives, local(): lax.all_to_all(reduced, 'node', split_axis=0, concat_axis=0, tiled=True)  4.84 us
    all_to_all x1, starting transfers between devices, local(): lax.all_to_all(partial_out, 'local', split_axis=1, concat_axis=1, tiled=T...  4.72 us
    all_to_all x1, blocking collectives, local(): lax.all_to_all(outgoing.reshape(node_count, per_node * CAP, model_width),...  4.27 us
  transfers between devices with their start and end apart: 1, of which 1 were waited for; matrix products, arithmetic and copies ran while one was open for 2% of the time, Pallas kernels for 0%

commit v1 on v0

v1 whole, which is shorter than its diff:
```python
import functools

import jax
import jax.numpy as jnp
from jax import lax
from jax.experimental import pallas as pl
from jax.experimental.pallas import tpu as pltpu
from jax.sharding import PartitionSpec as P

EXPERTS = 8
NC = 7
PAIR = 2

route_scale = 2.5
score_scale = 192.0 ** (-0.5)

MESH = pl.DeviceIdType.MESH
f32 = jnp.float32
bf16 = jnp.bfloat16


def kernel(
    nodes,
    locals_,
    hidden,
    router,
    chosen,
    w_gate,
    w_up,
    w_down,
    q_lat,
    q_rot,
    cache_lat,
    cache_rot,
    lengths,
    moe_out,
    context,
    rows,
    shares,
    gate_w,
    up_w,
    down_w,
    gate_acc,
    up_acc,
    inner,
    part,
    core_out,
    core_in,
    pair_sum,
    pair_out,
    pair_in,
    line_sum,
    line_out,
    line_in,
    gate_sem,
    up_sem,
    down_sem,
    dz_send,
    dz_recv,
    dy_send,
    dy_recv,
    dc_send,
    dc_recv,
    wz_send,
    wz_recv,
    w_send,
    w_recv,
    rz_send,
    rz_recv,
    ry_send,
    ry_recv,
    rc_send,
    rc_recv,
):
    line = locals_ // PAIR
    core = lax.axis_index("node")
    place = lax.axis_index("local")
    z = place // PAIR
    y = lax.rem(place, PAIR)
    expert = (core * locals_ + place) // (nodes * locals_ // EXPERTS)

    core_peer = {"node": 1 - core, "local": place}
    pair_peer = {"node": core, "local": z * PAIR + 1 - y}

    def ahead(d):
        return lax.rem(z + d, line)

    def line_peer(d):
        return {"node": core, "local": ahead(d) * PAIR + y}

    model_width = hidden.shape[1]
    ck = model_width // NC
    half = ck // 2
    ff = w_gate.shape[1]
    total = nodes * locals_ * 8

    def remote(src, dst, send, recv, peer):
        return pltpu.make_async_remote_copy(
            src_ref=src,
            dst_ref=dst,
            send_sem=send,
            recv_sem=recv,
            device_id=peer,
            device_id_type=MESH,
        )

    def load_gate(k):
        span = pl.ds(pl.multiple_of(k * ck, ck), ck)
        return pltpu.make_async_copy(w_gate.at[span, :], gate_w.at[k], gate_sem.at[k])

    def load_up(k):
        span = pl.ds(pl.multiple_of(k * ck, ck), ck)
        return pltpu.make_async_copy(w_up.at[span, :], up_w.at[k], up_sem.at[k])

    def load_down(k):
        span = pl.ds(pl.multiple_of(k * ck, ck), ck)
        return pltpu.make_async_copy(w_down.at[:, span], down_w.at[k], down_sem.at[k])

    def send_line(k, d):
        block = rows.at[k, core, y, z]
        return remote(block, block, dz_send.at[k, d - 1], dz_recv.at[k, d - 1], line_peer(d))

    def send_pair(k):
        block = rows.at[k, core, y]
        return remote(block, block, dy_send.at[k], dy_recv.at[k], pair_peer)

    def send_core(k):
        block = rows.at[k, core]
        return remote(block, block, dc_send.at[k], dc_recv.at[k], core_peer)

    def share_line(d):
        block = shares.at[core, y, z]
        return remote(block, block, wz_send.at[d - 1], wz_recv.at[d - 1], line_peer(d))

    def share_pair():
        block = shares.at[core, y]
        return remote(block, block, w_send.at[0], w_recv.at[0], pair_peer)

    def share_core():
        block = shares.at[core]
        return remote(block, block, w_send.at[1], w_recv.at[1], core_peer)

    def back_core(t):
        return remote(core_out.at[t], core_in.at[t], rc_send.at[t], rc_recv.at[t], core_peer)

    def back_pair(t):
        return remote(pair_out.at[t], pair_in.at[t], ry_send.at[t], ry_recv.at[t], pair_peer)

    def back_line(t, d):
        return remote(
            line_out.at[t, ahead(d)],
            line_in.at[t, d - 1],
            rz_send.at[t, d - 1],
            rz_recv.at[t, d - 1],
            line_peer(d),
        )

    barrier = pltpu.get_barrier_semaphore()
    peers = [core_peer, pair_peer] + [line_peer(d) for d in range(1, line)]
    for peer in peers:
        pl.semaphore_signal(barrier, inc=1, device_id=peer, device_id_type=MESH)

    for k in range(NC):
        load_gate(k).start()
        load_up(k).start()

    held = hidden[...].astype(f32)
    for k in range(NC):
        both = [held[:, k * ck + h * half : k * ck + (h + 1) * half] for h in range(2)]
        rows[k, core, y, z] = jnp.concatenate(both, axis=0).astype(bf16)

    pl.semaphore_wait(barrier, len(peers))
    for k in range(NC):
        for d in range(1, line):
            send_line(k, d).start()

    scores = jax.nn.sigmoid(jnp.dot(hidden[...], router[...], preferred_element_type=f32))
    slots = lax.broadcasted_iota(jnp.int32, (8, EXPERTS), 1)
    picked = jnp.zeros((8, EXPERTS), f32)
    for j in range(chosen.shape[1]):
        picked = picked + jnp.where(chosen[:, j : j + 1] == slots, scores, 0.0)
    weights = route_scale * picked / jnp.sum(picked, axis=1, keepdims=True)
    shares[core, y, z] = jnp.concatenate([weights, jnp.zeros((8, 128 - EXPERTS), f32)], axis=1)
    for d in range(1, line):
        share_line(d).start()

    gate_acc[...] = jnp.zeros_like(gate_acc)
    up_acc[...] = jnp.zeros_like(up_acc)

    def attend(b):
        logits = lax.dot_general(
            q_lat[b], cache_lat[b], (((1,), (1,)), ((), ())), preferred_element_type=f32
        )
        logits = logits + jnp.dot(q_rot[b], cache_rot[b], preferred_element_type=f32)
        logits = logits * score_scale
        usable = lax.broadcasted_iota(jnp.int32, logits.shape, 1) < lengths[b]
        logits = jnp.where(usable, logits, -1e30)
        raw = jnp.exp(logits - jnp.max(logits, axis=1, keepdims=True))
        probs = (raw / jnp.sum(raw, axis=1, keepdims=True)).astype(bf16)
        context[b] = jnp.dot(probs, cache_lat[b], preferred_element_type=f32).astype(bf16)

    batch = q_lat.shape[0]

    def gather_step(s, carry):
        @pl.when(s < NC)
        def _():
            for d in range(1, line):
                send_line(s, d).wait_recv()
            send_pair(s).start()
            load_down(s).start()

        @pl.when((s >= 1) & (s < NC + 1))
        def _():
            send_pair(s - 1).wait_recv()
            send_core(s - 1).start()

        @pl.when(s < batch)
        def _():
            attend(s)

        @pl.when(s == 3)
        def _():
            for d in range(1, line):
                share_line(d).wait_recv()
            share_pair().start()

        @pl.when(s == 5)
        def _():
            share_pair().wait_recv()
            share_core().start()

        @pl.when(s >= 2)
        def _():
            k = s - 2
            send_core(k).wait_recv()
            load_gate(k).wait()
            load_up(k).wait()
            block = rows[k].astype(f32).reshape(total // 8, 2, 8, half)
            x = jnp.concatenate(
                [block[:, h].reshape(total, half).astype(bf16) for h in range(2)], axis=1
            )
            gate_acc[...] += jnp.dot(x, gate_w[k], preferred_element_type=f32)
            up_acc[...] += jnp.dot(x, up_w[k], preferred_element_type=f32)

        return carry

    lax.fori_loop(0, NC + 2, gather_step, 0)

    gate = gate_acc[...]
    inner[...] = (gate / (1.0 + jnp.exp(-gate)) * up_acc[...]).astype(bf16)
    share_core().wait_recv()
    mine = lax.broadcasted_iota(jnp.int32, (total, 128), 1) == expert
    share = jnp.sum(
        jnp.where(mine, shares[...].reshape(total, 128), 0.0), axis=1, keepdims=True
    )
    gate_acc[...] = jnp.broadcast_to(share, gate_acc.shape)

    def return_step(t, carry):
        @pl.when(t < NC)
        def _():
            load_down(t).wait()
            p = jnp.dot(inner[...], down_w[t], preferred_element_type=f32)
            p = p * gate_acc[:, :1]
            for h in range(2):
                part[t, :, :, :, pl.ds(8 * h, 8), :] = p[:, h * half : (h + 1) * half].reshape(
                    nodes, PAIR, line, 8, half
                )
            core_out[t] = part[t, 1 - core].astype(bf16)
            back_core(t).start()

        @pl.when((t >= 1) & (t < NC + 1))
        def _():
            i = t - 1
            back_core(i).wait_recv()
            pair_sum[i] = part[i, core] + core_in[i].astype(f32)
            pair_out[i] = pair_sum[i, 1 - y].astype(bf16)
            back_pair(i).start()

        @pl.when((t >= 2) & (t < NC + 2))
        def _():
            i = t - 2
            back_pair(i).wait_recv()
            summed = pair_sum[i, y] + pair_in[i].astype(f32)
            line_sum[i] = summed
            line_out[i] = summed.astype(bf16)
            for d in range(1, line):
                back_line(i, d).start()

        @pl.when(t >= 3)
        def _():
            i = t - 3
            summed = line_sum[i, z]
            for d in range(1, line):
                back_line(i, d).wait_recv()
                summed = summed + line_in[i, d - 1].astype(f32)
            both = [summed[8 * h : 8 * h + 8] for h in range(2)]
            span = pl.ds(pl.multiple_of(i * ck, ck), ck)
            moe_out[:, span] = jnp.concatenate(both, axis=1).astype(bf16)

        return carry

    lax.fori_loop(0, NC + 3, return_step, 0)

    def drain(k, carry):
        for d in range(1, line):
            send_line(k, d).wait_send()
            back_line(k, d).wait_send()
        send_pair(k).wait_send()
        send_core(k).wait_send()
        back_pair(k).wait_send()
        back_core(k).wait_send()
        return carry

    lax.fori_loop(0, NC, drain, 0)
    for d in range(1, line):
        share_line(d).wait_send()
    share_pair().wait_send()
    share_core().wait_send()


def fused(
    nodes,
    locals_,
    hidden_rows,
    w_router,
    chosen,
    w_gate,
    w_up,
    w_down,
    q_latent,
    q_rope,
    cache_latent,
    cache_rope,
    lengths,
):
    batch_rows, positions, latent = cache_latent.shape
    rope_width = cache_rope.shape[1]
    heads = q_latent.shape[1] // latent
    row_count, model_width = hidden_rows.shape
    ff = w_gate.shape[1]
    line = locals_ // PAIR
    total = nodes * locals_ * row_count
    ck = model_width // NC
    half = ck // 2
    vmem = pl.BlockSpec(memory_space=pltpu.VMEM)
    hbm = pl.BlockSpec(memory_space=pl.ANY)
    smem = pl.BlockSpec(memory_space=pltpu.SMEM)
    dma = pltpu.SemaphoreType.DMA
    moe_out, context = pl.pallas_call(
        functools.partial(kernel, nodes, locals_),
        out_shape=(
            jax.ShapeDtypeStruct((row_count, model_width), bf16),
            jax.ShapeDtypeStruct((batch_rows, heads, latent), bf16),
        ),
        in_specs=[vmem, vmem, vmem, hbm, hbm, hbm, vmem, vmem, vmem, vmem, smem],
        out_specs=(vmem, vmem),
        scratch_shapes=[
            pltpu.VMEM((NC, nodes, PAIR, line, 16, half), bf16),
            pltpu.VMEM((nodes, PAIR, line, 8, 128), f32),
            pltpu.VMEM((NC, ck, ff), bf16),
            pltpu.VMEM((NC, ck, ff), bf16),
            pltpu.VMEM((NC, ff, ck), bf16),
            pltpu.VMEM((total, ff), f32),
            pltpu.VMEM((total, ff), f32),
            pltpu.VMEM((total, ff), bf16),
            pltpu.VMEM((NC, nodes, PAIR, line, 16, half), f32),
            pltpu.VMEM((NC, PAIR, line, 16, half), bf16),
            pltpu.VMEM((NC, PAIR, line, 16, half), bf16),
            pltpu.VMEM((NC, PAIR, line, 16, half), f32),
            pltpu.VMEM((NC, line, 16, half), bf16),
            pltpu.VMEM((NC, line, 16, half), bf16),
            pltpu.VMEM((NC, line, 16, half), f32),
            pltpu.VMEM((NC, line, 16, half), bf16),
            pltpu.VMEM((NC, line - 1, 16, half), bf16),
            dma((NC,)),
            dma((NC,)),
            dma((NC,)),
            dma((NC, line - 1)),
            dma((NC, line - 1)),
            dma((NC,)),
            dma((NC,)),
            dma((NC,)),
            dma((NC,)),
            dma((line - 1,)),
            dma((line - 1,)),
            dma((2,)),
            dma((2,)),
            dma((NC, line - 1)),
            dma((NC, line - 1)),
            dma((NC,)),
            dma((NC,)),
            dma((NC,)),
            dma((NC,)),
        ],
        compiler_params=pltpu.CompilerParams(
            collective_id=0, has_side_effects=True, vmem_limit_bytes=62 * 1024 * 1024
        ),
    )(
        hidden_rows,
        w_router,
        chosen,
        w_gate,
        w_up,
        w_down,
        q_latent.reshape(batch_rows, heads, latent),
        q_rope.reshape(batch_rows, heads, rope_width),
        cache_latent,
        cache_rope,
        lengths,
    )
    return moe_out, context.reshape(batch_rows, heads * latent)


def solution(mesh):
    nodes, locals_ = mesh.shape["node"], mesh.shape["local"]
    spread = ("rep", "node", "local")
    return jax.shard_map(
        functools.partial(fused, nodes, locals_),
        mesh=mesh,
        in_specs=(
            P(spread, None),
            P(),
            P(spread, None),
            P(None, ("node", "local")),
            P(None, ("node", "local")),
            P(("node", "local"), None),
            P(spread, None),
            P(spread, None),
            P(spread, None, None),
            P(spread, None, None),
            P(spread),
        ),
        out_specs=(P(spread, None), P(spread, None)),
        check_vma=False,
    )
```

time: 169 us -> 68 us (0.40)
  waiting for transfers between devices: 57.6 us -> 0 us
  Pallas kernels: 0 us -> 56.6 us
  blocking collectives: 49.9 us -> 0 us
  matrix products: 26 us -> 0 us
  local copies, waits for them, and re-layouts: 21 us -> 10.4 us
  other arithmetic: 8.04 us -> 0 us
  starting transfers between devices: 4.72 us -> 0 us
    all_to_all x1 -> x0, waiting for transfers between devices: 57.6 us -> none  [local(): lax.all_to_all(partial_out, 'local', split_axis=1, concat_axis=1, tiled=T...]
    pallas_call x0 -> x1, Pallas kernels: none -> 56.6 us  [fused(): pl.pallas_call(functools.partial(kernel, nodes, locals_), out_shape=(jax....]
    all_to_all x3 -> x0, blocking collectives: 49.9 us -> none  [the longest x1 40.8 us: local(): lax.all_to_all(fanned, 'local', split_axis=1, concat_axis=1, tiled=True)]
    dot_general x7 -> x0, matrix products: 26 us -> none  [the longest x1 15.7 us: expert_part(): partial_out = jnp.dot(inner_act, w_down, preferred_element_type=jnp.float32)]
    reshape x6 -> x1, local copies, waits for them, and re-layouts: 12.6 us -> 1.5 us  [fused(): q_rope.reshape(batch_rows, heads, rope_width)]
    unnamed x17 -> x5, local copies, waits for them, and re-layouts: 1.02 us -> 8.92 us
    reduce_sum x5 -> x0, other arithmetic: 6.9 us -> none  [the longest x1 3.59 us: local(): jnp.sum(returned.reshape(node_count, per_node, expert_span, slot_count, m...]
    all_to_all x1 -> x0, starting transfers between devices: 4.72 us -> none  [local(): lax.all_to_all(partial_out, 'local', split_axis=1, concat_axis=1, tiled=T...]
  transfers between devices with their start and end apart: 1 -> 0, of which waited for: 1 -> 0; matrix products, arithmetic and copies ran while one was open for 2% -> 0% of each run, Pallas kernels for 0% -> 0%
where the time goes in v1:
time: 68 us; the launch traced here: 67.7 us
  Pallas kernels  56.6 us (83%)
  local copies, waits for them, and re-layouts  10.4 us (15%)
    pallas_call x1, Pallas kernels, fused(): pl.pallas_call(functools.partial(kernel, nodes, locals_), out_shape=(jax....  56.6 us
    unnamed x5, local copies, waits for them, and re-layouts  8.92 us
    reshape x1, local copies, waits for them, and re-layouts, fused(): q_rope.reshape(batch_rows, heads, rope_width)  1.5 us

profile of v1, /device:TPU:0, one launch (start us, length us, event | category | flops | bytes accessed | tf_op | source)
XLA Modules:
  0.0 67.7 jit_solution(8469583137274290152)
XLA Ops:
  0.6 1.3 %copy.16.chosen = s32[8,4]{1,0:T(8,128)} copy(s32[8,4]{0,1:T(4,128)} %param.13) | data formatting | bytes 256 | tf_op args[2]
  2.0 1.5 %reshape.14.q_rot = bf16[2,128,64]{2,1,0:T(8,128)(2,1)} reshape(bf16[2,8192]{1,0:T(2,128)(2,1)} %param.18) | data formatting | bytes 65536 | tf_op jit(solution)/shard_map/reshape | solution.py:406
  3.5 1.7 %copy.20 = bf16[1,2,128,512]{3,2,1,0:T(8,128)(2,1)} copy(bf16[1,2,128,512]{3,1,2,0:T(2,128)(2,1)} %bitcast.7) | data formatting | bytes 524288
  5.2 2.4 %copy.15.router = bf16[7168,8]{1,0:T(8,128)(2,1)} copy(bf16[7168,8]{0,1:T(8,128)(2,1)} %param.12) | data formatting | bytes 229376 | tf_op args[1]
  7.6 56.6 %shard_map.122 = (bf16[8,7168]{1,0:T(8,128)(2,1)}, bf16[2,128,512]{2,1,0:T(8,128)(2,1)}) custom-call(bf16[8,7168]{1,0:T(8,128)(2,1)} %hidden.1, bf16[7168,8]{1,0:T(8,128)(2,1)} %copy.15.router, s32[8,4]{1,0:T(8,128)} %copy.16.chosen, bf16[7168,1024]{1,0:T(8,128)(2,1)} %w_gate.1, bf16[7168,1024]{1,0:T(8,128)(2,1)} %w_up.1, bf16[1024,7168]{1,0:T(8,128)(2,1)} %w_down.1, ...), custom_call_target="tpu_custom_call" | custom-call | tf_op jit(solution)/shard_map/pallas_call | solution.py:349
  64.2 1.9 %copy.18 = bf16[1,2,128,512]{3,1,2,0:T(2,128)(2,1)} copy(bf16[1,2,128,512]{3,2,1,0:T(8,128)(2,1)} %bitcast.9) | data formatting | bytes 524288
  66.1 1.6 %copy.22 = bf16[8,7168]{1,0:T(8,128)(2,1)} copy(bf16[8,7168]{1,0:T(8,128)(2,1)} %get-tuple-element.8) | data formatting | bytes 229376

commit v2 on v1

--- a/solution.py
+++ b/solution.py
@@ -10,6 +10,7 @@
 EXPERTS = 8
 NC = 7
 PAIR = 2
+LAG = 3
 
 route_scale = 2.5
 score_scale = 192.0 ** (-0.5)
@@ -28,13 +29,18 @@
     w_gate,
     w_up,
     w_down,
+    q_wide,
+    q_rot_wide,
+    cache_lat_hbm,
+    cache_rot_hbm,
+    lengths,
+    moe_out,
+    context,
     q_lat,
     q_rot,
     cache_lat,
     cache_rot,
-    lengths,
-    moe_out,
-    context,
+    summed_lat,
     rows,
     shares,
     gate_w,
@@ -52,6 +58,7 @@
     line_sum,
     line_out,
     line_in,
+    cache_sem,
     gate_sem,
     up_sem,
     down_sem,
@@ -160,6 +167,12 @@
     for peer in peers:
         pl.semaphore_signal(barrier, inc=1, device_id=peer, device_id_type=MESH)
 
+    caches = [
+        pltpu.make_async_copy(cache_lat_hbm, cache_lat, cache_sem.at[0]),
+        pltpu.make_async_copy(cache_rot_hbm, cache_rot, cache_sem.at[1]),
+    ]
+    for copy in caches:
+        copy.start()
     for k in range(NC):
         load_gate(k).start()
         load_up(k).start()
@@ -174,12 +187,17 @@
         for d in range(1, line):
             send_line(k, d).start()
 
-    scores = jax.nn.sigmoid(jnp.dot(hidden[...], router[...], preferred_element_type=f32))
-    slots = lax.broadcasted_iota(jnp.int32, (8, EXPERTS), 1)
-    picked = jnp.zeros((8, EXPERTS), f32)
-    for j in range(chosen.shape[1]):
-        picked = picked + jnp.where(chosen[:, j : j + 1] == slots, scores, 0.0)
-    weights = route_scale * picked / jnp.sum(picked, axis=1, keepdims=True)
+    scores = jax.nn.sigmoid(
+        lax.dot_general(
+            router[...], hidden[...], (((1,), (1,)), ((), ())), preferred_element_type=f32
+        )
+    )
+    slots = lax.broadcasted_iota(jnp.int32, (EXPERTS, 8), 0)
+    picked = jnp.zeros((EXPERTS, 8), f32)
+    for j in range(chosen.shape[0]):
+        picked = picked + jnp.where(chosen[j : j + 1, :] == slots, scores, 0.0)
+    weights = route_scale * picked / jnp.sum(picked, axis=0, keepdims=True)
+    weights = jnp.concatenate([weights, jnp.zeros((EXPERTS, 120), f32)], axis=1).T[:8]
     shares[core, y, z] = jnp.concatenate([weights, jnp.zeros((8, 128 - EXPERTS), f32)], axis=1)
     for d in range(1, line):
         share_line(d).start()
@@ -197,9 +215,37 @@
         logits = jnp.where(usable, logits, -1e30)
         raw = jnp.exp(logits - jnp.max(logits, axis=1, keepdims=True))
         probs = (raw / jnp.sum(raw, axis=1, keepdims=True)).astype(bf16)
-        context[b] = jnp.dot(probs, cache_lat[b], preferred_element_type=f32).astype(bf16)
-
-    batch = q_lat.shape[0]
+        summed_lat[b] = jnp.dot(probs, cache_lat[b], preferred_element_type=f32)
+
+    batch, heads, latent = q_lat.shape
+    rope = q_rot.shape[2]
+
+    def spread_queries():
+        def group(g, carry):
+            first = pl.multiple_of(g * 16, 16)
+            lat = q_wide[:, pl.ds(pl.multiple_of(g * 16 * latent, 128), 16 * latent)].astype(f32)
+            rot = q_rot_wide[:, pl.ds(pl.multiple_of(g * 16 * rope, 128), 16 * rope)].astype(f32)
+            for b in range(batch):
+                picks = [lat[b : b + 1, h * latent : (h + 1) * latent] for h in range(16)]
+                q_lat[b, pl.ds(first, 16), :] = jnp.concatenate(picks, axis=0).astype(bf16)
+                picks = [rot[b : b + 1, h * rope : (h + 1) * rope] for h in range(16)]
+                q_rot[b, pl.ds(first, 16), :] = jnp.concatenate(picks, axis=0).astype(bf16)
+            return carry
+
+        lax.fori_loop(0, heads // 16, group, 0)
+
+    def join_context():
+        def group(g, carry):
+            first = pl.multiple_of(g * 8, 8)
+            parts = [summed_lat[b, pl.ds(first, 8), :] for b in range(batch)]
+            both = [
+                jnp.concatenate([v[h : h + 1] for v in parts], axis=0) for h in range(8)
+            ]
+            span = pl.ds(pl.multiple_of(g * 8 * latent, 128), 8 * latent)
+            context[:, span] = jnp.concatenate(both, axis=1).astype(bf16)
+            return carry
+
+        lax.fori_loop(0, heads // 8, group, 0)
 
     def gather_step(s, carry):
         @pl.when(s < NC)
@@ -209,29 +255,39 @@
             send_pair(s).start()
             load_down(s).start()
 
-        @pl.when((s >= 1) & (s < NC + 1))
-        def _():
-            send_pair(s - 1).wait_recv()
-            send_core(s - 1).start()
-
-        @pl.when(s < batch)
-        def _():
-            attend(s)
-
-        @pl.when(s == 3)
+        @pl.when((s >= LAG) & (s < NC + LAG))
+        def _():
+            send_pair(s - LAG).wait_recv()
+            send_core(s - LAG).start()
+
+        @pl.when(s == 0)
+        def _():
+            for copy in caches:
+                copy.wait()
+            spread_queries()
+
+        @pl.when((s >= 1) & (s <= batch))
+        def _():
+            attend(s - 1)
+
+        @pl.when(s == batch + 1)
+        def _():
+            join_context()
+
+        @pl.when(s == 5)
         def _():
             for d in range(1, line):
                 share_line(d).wait_recv()
             share_pair().start()
 
-        @pl.when(s == 5)
+        @pl.when(s == 8)
         def _():
             share_pair().wait_recv()
             share_core().start()
 
-        @pl.when(s >= 2)
-        def _():
-            k = s - 2
+        @pl.when(s > LAG)
+        def _():
+            k = s - LAG - 1
             send_core(k).wait_recv()
             load_gate(k).wait()
             load_up(k).wait()
@@ -244,7 +300,7 @@
 
         return carry
 
-    lax.fori_loop(0, NC + 2, gather_step, 0)
+    lax.fori_loop(0, NC + LAG + 1, gather_step, 0)
 
     gate = gate_acc[...]
     inner[...] = (gate / (1.0 + jnp.exp(-gate)) * up_acc[...]).astype(bf16)
@@ -261,24 +317,28 @@
             load_down(t).wait()
             p = jnp.dot(inner[...], down_w[t], preferred_element_type=f32)
             p = p * gate_acc[:, :1]
+            p = p.reshape(nodes, total // nodes, ck)
+            keep = jnp.where(core == 0, p[0], p[1])
+            give = jnp.where(core == 0, p[1], p[0])
             for h in range(2):
-                part[t, :, :, :, pl.ds(8 * h, 8), :] = p[:, h * half : (h + 1) * half].reshape(
-                    nodes, PAIR, line, 8, half
-                )
-            core_out[t] = part[t, 1 - core].astype(bf16)
+                span = slice(h * half, (h + 1) * half)
+                part[t, :, :, pl.ds(8 * h, 8), :] = keep[:, span].reshape(PAIR, line, 8, half)
+            give = [give[:, h * half : (h + 1) * half] for h in range(2)]
+            give = [v.reshape(PAIR, line, 8, half) for v in give]
+            core_out[t] = jnp.concatenate(give, axis=2).astype(bf16)
             back_core(t).start()
 
         @pl.when((t >= 1) & (t < NC + 1))
         def _():
             i = t - 1
             back_core(i).wait_recv()
-            pair_sum[i] = part[i, core] + core_in[i].astype(f32)
+            pair_sum[i] = part[i] + core_in[i].astype(f32)
             pair_out[i] = pair_sum[i, 1 - y].astype(bf16)
             back_pair(i).start()
 
-        @pl.when((t >= 2) & (t < NC + 2))
-        def _():
-            i = t - 2
+        @pl.when((t >= 1 + LAG) & (t < NC + 1 + LAG))
+        def _():
+            i = t - 1 - LAG
             back_pair(i).wait_recv()
             summed = pair_sum[i, y] + pair_in[i].astype(f32)
             line_sum[i] = summed
@@ -286,9 +346,9 @@
             for d in range(1, line):
                 back_line(i, d).start()
 
-        @pl.when(t >= 3)
-        def _():
-            i = t - 3
+        @pl.when(t >= 1 + 2 * LAG)
+        def _():
+            i = t - 1 - 2 * LAG
             summed = line_sum[i, z]
             for d in range(1, line):
                 back_line(i, d).wait_recv()
@@ -299,7 +359,7 @@
 
         return carry
 
-    lax.fori_loop(0, NC + 3, return_step, 0)
+    lax.fori_loop(0, NC + 1 + 2 * LAG, return_step, 0)
 
     def drain(k, carry):
         for d in range(1, line):
@@ -350,11 +410,16 @@
         functools.partial(kernel, nodes, locals_),
         out_shape=(
             jax.ShapeDtypeStruct((row_count, model_width), bf16),
-            jax.ShapeDtypeStruct((batch_rows, heads, latent), bf16),
+            jax.ShapeDtypeStruct((batch_rows, heads * latent), bf16),
         ),
-        in_specs=[vmem, vmem, vmem, hbm, hbm, hbm, vmem, vmem, vmem, vmem, smem],
+        in_specs=[vmem, vmem, vmem, hbm, hbm, hbm, vmem, vmem, hbm, hbm, smem],
         out_specs=(vmem, vmem),
         scratch_shapes=[
+            pltpu.VMEM((batch_rows, heads, latent), bf16),
+            pltpu.VMEM((batch_rows, heads, rope_width), bf16),
+            pltpu.VMEM(cache_latent.shape, bf16),
+            pltpu.VMEM(cache_rope.shape, bf16),
+            pltpu.VMEM((batch_rows, heads, latent), f32),
             pltpu.VMEM((NC, nodes, PAIR, line, 16, half), bf16),
             pltpu.VMEM((nodes, PAIR, line, 8, 128), f32),
             pltpu.VMEM((NC, ck, ff), bf16),
@@ -363,7 +428,7 @@
             pltpu.VMEM((total, ff), f32),
             pltpu.VMEM((total, ff), f32),
             pltpu.VMEM((total, ff), bf16),
-            pltpu.VMEM((NC, nodes, PAIR, line, 16, half), f32),
+            pltpu.VMEM((NC, PAIR, line, 16, half), f32),
             pltpu.VMEM((NC, PAIR, line, 16, half), bf16),
             pltpu.VMEM((NC, PAIR, line, 16, half), bf16),
             pltpu.VMEM((NC, PAIR, line, 16, half), f32),
@@ -372,6 +437,7 @@
             pltpu.VMEM((NC, line, 16, half), f32),
             pltpu.VMEM((NC, line, 16, half), bf16),
             pltpu.VMEM((NC, line - 1, 16, half), bf16),
+            dma((2,)),
             dma((NC,)),
             dma((NC,)),
             dma((NC,)),
@@ -397,18 +463,18 @@
         ),
     )(
         hidden_rows,
-        w_router,
-        chosen,
+        w_router.T,
+        chosen.T,
         w_gate,
         w_up,
         w_down,
-        q_latent.reshape(batch_rows, heads, latent),
-        q_rope.reshape(batch_rows, heads, rope_width),
+        q_latent,
+        q_rope,
         cache_latent,
         cache_rope,
         lengths,
     )
-    return moe_out, context.reshape(batch_rows, heads * latent)
+    return moe_out, context
 
 
 def solution(mesh):

time: 68 us -> 50.1 us (0.74)
  Pallas kernels: 56.6 us -> 45.9 us
  local copies, waits for them, and re-layouts: 10.4 us -> 3.38 us
    pallas_call x1, Pallas kernels: 56.6 us -> 45.9 us  [fused(): pl.pallas_call(functools.partial(kernel, nodes, locals_), out_shape=(jax....]
    unnamed x5 -> x2, local copies, waits for them, and re-layouts: 8.92 us -> 3.38 us
    reshape x1 -> x0, local copies, waits for them, and re-layouts: 1.5 us -> none  [fused(): q_rope.reshape(batch_rows, heads, rope_width)]
where the time goes in v2:
time: 50.1 us; the launch traced here: 49.9 us
  Pallas kernels  45.9 us (92%)
  local copies, waits for them, and re-layouts  3.38 us (7%)
  between operations  0.64 us (1%)
    pallas_call x1, Pallas kernels, fused(): pl.pallas_call(functools.partial(kernel, nodes, locals_), out_shape=(jax....  45.9 us
    unnamed x2, local copies, waits for them, and re-layouts  3.38 us

profile of v2, /device:TPU:0, one launch (start us, length us, event | category | flops | bytes accessed | tf_op | source)
XLA Modules:
  0.0 49.9 jit_solution(16143157632335564456)
XLA Ops:
  0.6 45.9 %shard_map.122 = (bf16[8,7168]{1,0:T(8,128)(2,1)}, bf16[2,65536]{1,0:T(2,128)(2,1)}) custom-call(bf16[8,7168]{1,0:T(8,128)(2,1)} %hidden.1, bf16[8,7168]{1,0:T(8,128)(2,1)} %bitcast.2, s32[4,8]{1,0:T(4,128)} %bitcast.3, bf16[7168,1024]{1,0:T(8,128)(2,1)} %w_gate.1, bf16[7168,1024]{1,0:T(8,128)(2,1)} %w_up.1, bf16[1024,7168]{1,0:T(8,128)(2,1)} %w_down.1, ...), custom_call_target="tpu_custom_call" | custom-call | tf_op jit(solution)/shard_map/pallas_call | solution.py:409
  46.5 1.6 %copy.15 = bf16[8,7168]{1,0:T(8,128)(2,1)} copy(bf16[8,7168]{1,0:T(8,128)(2,1)} %get-tuple-element.4) | data formatting | bytes 229376
  48.1 1.8 %copy.16 = bf16[2,65536]{1,0:T(2,128)(2,1)} copy(bf16[2,65536]{1,0:T(2,128)(2,1)} %get-tuple-element.5) | data formatting | bytes 524288

commit v3 on v2

--- a/solution.py
+++ b/solution.py
@@ -11,6 +11,9 @@
 NC = 7
 PAIR = 2
 LAG = 3
+CORE_LAG = 1
+BACK_CORE = 1
+BACK_LAG = 3
 
 route_scale = 2.5
 score_scale = 192.0 ** (-0.5)
@@ -285,9 +288,9 @@
             share_pair().wait_recv()
             share_core().start()
 
-        @pl.when(s > LAG)
-        def _():
-            k = s - LAG - 1
+        @pl.when(s >= LAG + CORE_LAG)
+        def _():
+            k = s - LAG - CORE_LAG
             send_core(k).wait_recv()
             load_gate(k).wait()
             load_up(k).wait()
@@ -300,7 +303,7 @@
 
         return carry
 
-    lax.fori_loop(0, NC + LAG + 1, gather_step, 0)
+    lax.fori_loop(0, NC + LAG + CORE_LAG, gather_step, 0)
 
     gate = gate_acc[...]
     inner[...] = (gate / (1.0 + jnp.exp(-gate)) * up_acc[...]).astype(bf16)
@@ -328,17 +331,17 @@
             core_out[t] = jnp.concatenate(give, axis=2).astype(bf16)
             back_core(t).start()
 
-        @pl.when((t >= 1) & (t < NC + 1))
-        def _():
-            i = t - 1
+        @pl.when((t >= BACK_CORE) & (t < NC + BACK_CORE))
+        def _():
+            i = t - BACK_CORE
             back_core(i).wait_recv()
             pair_sum[i] = part[i] + core_in[i].astype(f32)
             pair_out[i] = pair_sum[i, 1 - y].astype(bf16)
             back_pair(i).start()
 
-        @pl.when((t >= 1 + LAG) & (t < NC + 1 + LAG))
-        def _():
-            i = t - 1 - LAG
+        @pl.when((t >= BACK_CORE + BACK_LAG) & (t < NC + BACK_CORE + BACK_LAG))
+        def _():
+            i = t - BACK_CORE - BACK_LAG
             back_pair(i).wait_recv()
             summed = pair_sum[i, y] + pair_in[i].astype(f32)
             line_sum[i] = summed
@@ -346,9 +349,9 @@
             for d in range(1, line):
                 back_line(i, d).start()
 
-        @pl.when(t >= 1 + 2 * LAG)
-        def _():
-            i = t - 1 - 2 * LAG
+        @pl.when(t >= BACK_CORE + 2 * BACK_LAG)
+        def _():
+            i = t - BACK_CORE - 2 * BACK_LAG
             summed = line_sum[i, z]
             for d in range(1, line):
                 back_line(i, d).wait_recv()
@@ -359,7 +362,7 @@
 
         return carry
 
-    lax.fori_loop(0, NC + 1 + 2 * LAG, return_step, 0)
+    lax.fori_loop(0, NC + BACK_CORE + 2 * BACK_LAG, return_step, 0)
 
     def drain(k, carry):
         for d in range(1, line):
@@ -376,6 +379,17 @@
         share_line(d).wait_send()
     share_pair().wait_send()
     share_core().wait_send()
+
+
+def place_outputs(moe, context, moe_out, context_out, sems):
+    copies = [
+        pltpu.make_async_copy(moe, moe_out, sems.at[0]),
+        pltpu.make_async_copy(context, context_out, sems.at[1]),
+    ]
+    for copy in copies:
+        copy.start()
+    for copy in copies:
+        copy.wait()
 
 
 def fused(
@@ -474,7 +488,16 @@
         cache_rope,
         lengths,
     )
-    return moe_out, context
+    return pl.pallas_call(
+        place_outputs,
+        out_shape=(
+            jax.ShapeDtypeStruct(moe_out.shape, bf16),
+            jax.ShapeDtypeStruct(context.shape, bf16),
+        ),
+        in_specs=[hbm, hbm],
+        out_specs=(vmem, vmem),
+        scratch_shapes=[dma((2,))],
+    )(moe_out, context)
 
 
 def solution(mesh):

time: 50.1 us -> 48.5 us (0.968)
  local copies, waits for them, and re-layouts: 3.38 us -> 0 us
  Pallas kernels: 45.9 us -> 47.7 us
    unnamed x2 -> x0, local copies, waits for them, and re-layouts: 3.38 us -> none
    pallas_call x0 -> x1, Pallas kernels: none -> 1.77 us  [fused(): pl.pallas_call(place_outputs, out_shape=(jax.ShapeDtypeStruct(moe_out.sha...]
where the time goes in v3:
time: 48.5 us; the launch traced here: 48.3 us
  Pallas kernels  47.7 us (98%)
  between operations  0.64 us (1%)
    pallas_call x1, Pallas kernels, fused(): pl.pallas_call(functools.partial(kernel, nodes, locals_), out_shape=(jax....  45.9 us
    pallas_call x1, Pallas kernels, fused(): pl.pallas_call(place_outputs, out_shape=(jax.ShapeDtypeStruct(moe_out.sha...  1.77 us

profile of v3, /device:TPU:0, one launch (start us, length us, event | category | flops | bytes accessed | tf_op | source)
XLA Modules:
  0.0 48.3 jit_solution(373995436150062205)
XLA Ops:
  0.6 45.9 %shard_map.122 = (bf16[8,7168]{1,0:T(8,128)(2,1)}, bf16[2,65536]{1,0:T(2,128)(2,1)}) custom-call(bf16[8,7168]{1,0:T(8,128)(2,1)} %hidden.1, bf16[8,7168]{1,0:T(8,128)(2,1)} %bitcast.2, s32[4,8]{1,0:T(4,128)} %bitcast.3, bf16[7168,1024]{1,0:T(8,128)(2,1)} %w_gate.1, bf16[7168,1024]{1,0:T(8,128)(2,1)} %w_up.1, bf16[1024,7168]{1,0:T(8,128)(2,1)} %w_down.1, ...), custom_call_target="tpu_custom_call" | custom-call | tf_op jit(solution)/shard_map/pallas_call | solution.py:423
  46.5 1.8 %shard_map.123 = (bf16[8,7168]{1,0:T(8,128)(2,1)}, bf16[2,65536]{1,0:T(2,128)(2,1)}) custom-call(bf16[8,7168]{1,0:T(8,128)(2,1)} %get-tuple-element.4.moe, bf16[2,65536]{1,0:T(2,128)(2,1)} %get-tuple-element.5.context), custom_call_target="tpu_custom_call" | custom-call | tf_op jit(solution)/shard_map/pallas_call | solution.py:491

commit v4 on v3

--- a/solution.py
+++ b/solution.py
@@ -176,9 +176,6 @@
     ]
     for copy in caches:
         copy.start()
-    for k in range(NC):
-        load_gate(k).start()
-        load_up(k).start()
 
     held = hidden[...].astype(f32)
     for k in range(NC):
@@ -189,6 +186,9 @@
     for k in range(NC):
         for d in range(1, line):
             send_line(k, d).start()
+    for k in range(NC):
+        load_gate(k).start()
+        load_up(k).start()
 
     scores = jax.nn.sigmoid(
         lax.dot_general(

time: 48.5 us -> 47.7 us (0.984)
  Pallas kernels: 47.7 us -> 46.9 us
    pallas_call x1, Pallas kernels: 45.9 us -> 45.1 us  [fused(): pl.pallas_call(functools.partial(kernel, nodes, locals_), out_shape=(jax....]
where the time goes in v4:
time: 47.7 us; the launch traced here: 47.6 us
  Pallas kernels  46.9 us (98%)
  between operations  0.64 us (1%)
    pallas_call x1, Pallas kernels, fused(): pl.pallas_call(functools.partial(kernel, nodes, locals_), out_shape=(jax....  45.1 us
    pallas_call x1, Pallas kernels, fused(): pl.pallas_call(place_outputs, out_shape=(jax.ShapeDtypeStruct(moe_out.sha...  1.77 us

profile of v4, /device:TPU:0, one launch (start us, length us, event | category | flops | bytes accessed | tf_op | source)
XLA Modules:
  0.0 47.6 jit_solution(5328109083129090579)
XLA Ops:
  0.6 45.1 %shard_map.122 = (bf16[8,7168]{1,0:T(8,128)(2,1)}, bf16[2,65536]{1,0:T(2,128)(2,1)}) custom-call(bf16[8,7168]{1,0:T(8,128)(2,1)} %hidden.1, bf16[8,7168]{1,0:T(8,128)(2,1)} %bitcast.2, s32[4,8]{1,0:T(4,128)} %bitcast.3, bf16[7168,1024]{1,0:T(8,128)(2,1)} %w_gate.1, bf16[7168,1024]{1,0:T(8,128)(2,1)} %w_up.1, bf16[1024,7168]{1,0:T(8,128)(2,1)} %w_down.1, ...), custom_call_target="tpu_custom_call" | custom-call | tf_op jit(solution)/shard_map/pallas_call | solution.py:423
  45.8 1.8 %shard_map.123 = (bf16[8,7168]{1,0:T(8,128)(2,1)}, bf16[2,65536]{1,0:T(2,128)(2,1)}) custom-call(bf16[8,7168]{1,0:T(8,128)(2,1)} %get-tuple-element.4.moe, bf16[2,65536]{1,0:T(2,128)(2,1)} %get-tuple-element.5.context), custom_call_target="tpu_custom_call" | custom-call | tf_op jit(solution)/shard_map/pallas_call | solution.py:491
